TPU v7x, 32 devices: a whole 2x2x4 slice. The times are simulated.
32 devices in a mesh: dp: 8 (over y, x, core), pipe: 4 (over z).
Axes of the slice: x: 2, y: 2, z: 4, core: 2. Of those that a mesh axis runs over, the one named last changes fastest.
Arguments:
- fwd_x: bfloat16 [4, 8, 64, 3584], P('pipe', 'dp'), may hold values from -6 to 6
- fwd_q: bfloat16 [4, 8, 64, 3584], P('pipe', 'dp')
- bwd_x: bfloat16 [4, 8, 64, 3584], P('pipe', 'dp'), may hold values from -6 to 6
- bwd_q: bfloat16 [4, 8, 64, 3584], P('pipe', 'dp')
- bwd_dout: bfloat16 [4, 8, 64, 3584], P('pipe', 'dp'), may hold values from -6 to 6
- cache_kv: bfloat16 [4, 8, 1024, 1024], P('pipe', 'dp'), may hold values from -6 to 6
- kv_weight: bfloat16 [4, 3584, 1024], P('pipe', 'dp'), may hold values from -0.09375 to 0.09375
- seg_lengths: int32 [4, 8, 4], P('pipe', 'dp'), may hold values from 1 to 896, as said below
Outputs:
- next_act: bfloat16 [4, 8, 64, 3584], P('pipe', 'dp')
- grad_q: bfloat16 [4, 8, 64, 3584], P('pipe', 'dp')
- prev_grad: bfloat16 [4, 8, 64, 3584], P('pipe', 'dp')
- weight_grad: float32 [4, 3584, 1024], P('pipe', 'dp')
Inputs may be any that keep to these rules, and one draw needn't show every extreme that they name: `seg_lengths`: each row holds four lengths that sum to 1024; the first is at least 1; the second lies from 64 to 127 and is 64 in some row of every draw; the third is at most 64 and equals 64 in some row of every draw; the fourth lies from 32 to the third.
All inputs are finite; a program needn't handle non-finite values.
Results may differ from a plain program's by a relative error of at most 0.035.
Values may be sent and summed in bfloat16 or wider, within the bound.
A program may use at most 128 MiB of HBM per device.

v0:
```python
import math

import jax
import jax.numpy as jnp
from jax import lax
from jax.sharding import PartitionSpec as P

HD = 128


def shifted(value, axis, steps):
    count = lax.axis_size(axis)
    first, last = (max(0, -steps), min(count, count - steps))
    return lax.ppermute(value, axis, [(source, source + steps) for source in range(first, last)])


def masked_softmax(scores, allowed):
    masked = jnp.where(allowed[:, None, :], scores, -1e30)
    top = jnp.max(masked, axis=-1, keepdims=True)
    raised = jnp.exp(masked - top)
    return raised / jnp.sum(raised, axis=-1, keepdims=True)


def forward_segment(query, own_kv, cache, length):
    seg = query.shape[0]
    seq_len = cache.shape[0]
    half = cache.shape[1] // 2
    kv_heads = half // HD
    group = query.shape[1] // half
    scale = 1.0 / math.sqrt(HD)
    start = seq_len - length
    rows = jnp.arange(seg, dtype=jnp.int32)
    cache_ok = jnp.broadcast_to(
        jnp.arange(seq_len, dtype=jnp.int32)[None, :] < start, (seg, seq_len)
    )
    own_ok = (rows[None, :] <= rows[:, None]) & (rows[None, :] < length)
    allowed = jnp.concatenate([cache_ok, own_ok], axis=1)
    keys = jnp.concatenate([cache[:, :half], own_kv[:, :half]], axis=0)
    values = jnp.concatenate([cache[:, half:], own_kv[:, half:]], axis=0)
    pieces = []
    for head in range(kv_heads):
        block = query[:, head * group * HD : (head + 1) * group * HD].reshape(seg * group, HD)
        key_head = keys[:, head * HD : (head + 1) * HD]
        scores = (jnp.dot(block, key_head.T, preferred_element_type=jnp.float32) * scale).reshape(
            seg, group, -1
        )
        probs = masked_softmax(scores, allowed).astype(jnp.bfloat16).reshape(seg * group, -1)
        mixed = jnp.dot(
            probs, values[:, head * HD : (head + 1) * HD], preferred_element_type=jnp.float32
        )
        pieces.append(mixed.reshape(seg, group * HD))
    result = jnp.concatenate(pieces, axis=1)
    return jnp.where((rows < length)[:, None], result, 0.0).astype(jnp.bfloat16)


def backward_segment(query, dout, cache, third, fourth):
    seg = query.shape[0]
    seq_len = cache.shape[0]
    half = cache.shape[1] // 2
    kv_heads = half // HD
    group = query.shape[1] // half
    scale = 1.0 / math.sqrt(HD)
    start = seq_len - fourth - third
    rows = jnp.arange(seg, dtype=jnp.int32)
    allowed = jnp.arange(seq_len, dtype=jnp.int32)[None, :] <= start + rows[:, None]
    live = (rows < third)[:, None]
    dout = jnp.where(live, dout, jnp.zeros_like(dout))
    query_parts, key_parts, value_parts = ([], [], [])
    for head in range(kv_heads):
        block = query[:, head * group * HD : (head + 1) * group * HD].reshape(seg * group, HD)
        grad_block = dout[:, head * group * HD : (head + 1) * group * HD].reshape(seg * group, HD)
        key_head = cache[:, head * HD : (head + 1) * HD]
        value_head = cache[:, half + head * HD : half + (head + 1) * HD]
        scores = (jnp.dot(block, key_head.T, preferred_element_type=jnp.float32) * scale).reshape(
            seg, group, seq_len
        )
        probs = masked_softmax(scores, allowed).reshape(seg * group, seq_len)
        rounded = probs.astype(jnp.bfloat16)
        mixed = jnp.dot(rounded, value_head, preferred_element_type=jnp.float32)
        delta = jnp.sum(grad_block.astype(jnp.float32) * mixed, axis=1, keepdims=True)
        along = jnp.dot(grad_block, value_head.T, preferred_element_type=jnp.float32)
        dscore = (probs * (along - delta)).astype(jnp.bfloat16)
        query_parts.append(
            (jnp.dot(dscore, key_head, preferred_element_type=jnp.float32) * scale).reshape(
                seg, group * HD
            )
        )
        dscore_own = lax.dynamic_slice_in_dim(dscore, start, seg, 1)
        rounded_own = lax.dynamic_slice_in_dim(rounded, start, seg, 1)
        key_parts.append(jnp.dot(dscore_own.T, block, preferred_element_type=jnp.float32) * scale)
        value_parts.append(jnp.dot(rounded_own.T, grad_block, preferred_element_type=jnp.float32))
    grad_query = jnp.concatenate(query_parts, axis=1).astype(jnp.bfloat16)
    kv_grad = jnp.concatenate(key_parts + value_parts, axis=1)
    kv_grad = jnp.where(live, kv_grad, 0.0).astype(jnp.bfloat16)
    return (grad_query, kv_grad)


def shards(fwd_x, fwd_q, bwd_x, bwd_q, bwd_dout, cache_kv, kv_weight, seg_lengths):
    front_x = fwd_x[0, 0]
    front_q = fwd_q[0, 0]
    back_x = bwd_x[0, 0]
    back_q = bwd_q[0, 0]
    back_dout = bwd_dout[0, 0]
    cache = cache_kv[0, 0]
    shard = kv_weight[0]
    lengths = seg_lengths[0, 0]
    columns = front_x
    own_kv = jnp.dot(
        columns, lax.all_gather(shard, "dp", axis=0, tiled=True), preferred_element_type=jnp.float32
    ).astype(jnp.bfloat16)
    fwd_out = forward_segment(front_q, own_kv, cache, lengths[3])
    grad_query, kv_grad = backward_segment(back_q, back_dout, cache, lengths[2], lengths[3])
    input_grad = jnp.dot(
        kv_grad,
        lax.all_gather(shard, "dp", axis=0, tiled=True).T,
        preferred_element_type=jnp.float32,
    ).astype(jnp.bfloat16)
    columns = back_x
    weight_grad = lax.psum_scatter(
        jnp.dot(columns.T, kv_grad, preferred_element_type=jnp.float32),
        "dp",
        scatter_dimension=0,
        tiled=True,
    )
    next_act = shifted(fwd_out, "pipe", 1)
    prev_grad = shifted(input_grad, "pipe", -1)
    return (next_act[None, None], grad_query[None, None], prev_grad[None, None], weight_grad[None])


def solution(mesh):
    return jax.shard_map(
        shards,
        mesh=mesh,
        in_specs=(
            P("pipe", "dp", None, None),
            P("pipe", "dp", None, None),
            P("pipe", "dp", None, None),
            P("pipe", "dp", None, None),
            P("pipe", "dp", None, None),
            P("pipe", "dp", None, None),
            P("pipe", "dp", None),
            P("pipe", "dp", None),
        ),
        out_specs=(
            P("pipe", "dp", None, None),
            P("pipe", "dp", None, None),
            P("pipe", "dp", None, None),
            P("pipe", "dp", None),
        ),
        check_vma=False,
    )
```

profile of v0, /device:TPU:0, one launch (start us, length us, event | category | flops | bytes accessed | tf_op | source)
XLA Modules:
  0.0 182.8 jit_solution(16977379173309838805)
XLA Ops:
  7.2 0.7 all-gather.3.cloned.1.call-update
  8.0 1.4 fusion.113
  11.3 0.7 iota_compare_fusion.3
  12.2 0.8 reshape.317
  12.9 0.8 reshape.323
  13.7 0.8 reshape.321
  14.5 0.8 reshape.319
  15.3 1.7 fusion.109
  17.4 1.0 reshape.318
  18.5 0.6 fusion.120
  19.1 0.5 fusion.22
  19.9 0.5 copy-done.11
  20.5 0.5 fusion.35
  21.0 0.6 fusion.119
  21.5 0.5 fusion.24
  22.4 0.5 copy-done.9
  22.9 0.5 fusion.36
  23.4 0.6 fusion.118
  24.9 0.5 copy-done.8
  25.4 0.5 fusion.37
  25.9 0.6 fusion.121
  27.3 0.5 copy-done.10
  27.8 0.5 fusion.34
  28.3 0.6 multiply_convert_fusion.3
  29.2 0.6 multiply_convert_fusion.2
  30.2 0.6 multiply_convert_fusion.1
  31.1 0.6 multiply_convert_fusion
  33.3 0.7 copy-done.4
  34.0 8.4 %convolution_bitcast_fusion = f32[3584,1024]{0,1:T(8,128)} fusion(bf16[1,1,64,3584]{3,2,1,0:T(8,128)(2,1)S(1)} %copy-done, bf16[64,1024]{1,0:T(8,128)(2,1)S(1)} %convolution_dynamic-update-slice_fusion, pred[64]{0:T(512)(128)(4,1)S(1)} %iota_compare_fusion.3), kind=kOutput, calls=%fused_computation | convolution fusion | flops 469827584 | bytes 15269952 | tf_op jit(solution)/shard_map/dot_general | solution.py:120
  42.4 15.4 %copy.15 = f32[3584,1024]{1,0:T(8,128)} copy(f32[3584,1024]{0,1:T(8,128)} %convolution_bitcast_fusion) | data formatting | bytes 29360128
  57.8 1.0 copy-done.7
  58.8 0.8 reshape.308
  59.7 0.8 reshape.312
  60.5 0.8 reshape.310
  61.3 0.6 iota_compare_fusion.4
  62.0 1.1 broadcast_in_dim.140
  63.1 1.6 broadcast_in_dim.141
  64.7 1.6 fusion.31
  66.4 1.6 fusion.32
  68.2 1.6 fusion.33
  69.9 1.6 fusion.30
  71.6 1.9 %fusion.108 = (bf16[1024,512]{1,0:T(8,128)(2,1)S(1)}, bf16[1024,512]{1,0:T(8,128)(2,1)S(1)}) fusion(bf16[1024,1024]{1,0:T(8,128)(2,1)} %bitcast.73), kind=kLoop, calls=%fused_computation.164 | loop fusion | bytes 4194304 | tf_op jit(solution)/shard_map/slice | solution.py:39
  73.6 8.2 %fusion.4 = bf16[64,3584]{1,0:T(8,128)(2,1)} fusion(bf16[1,3584,1024]{2,1,0:T(8,128)(2,1)} %all-gather.3.cloned.1.call-done, bf16[64,1024]{1,0:T(8,128)(2,1)S(1)} %copy-done.5, pred[64]{0:T(512)(128)(4,1)S(1)} %iota_compare_fusion.3), kind=kOutput, calls=%fused_computation.5 | convolution fusion | flops 470056960 | bytes 7929920 | tf_op jit(solution)/shard_map/dot_general | solution.py:113
  81.8 1.6 collective-permute-start.1
  83.5 1.4 fusion.27
  84.9 0.6 fusion.117
  86.0 1.2 fusion.42
  87.2 1.0 reshape.309
  88.3 0.6 fusion.116
  89.8 1.2 fusion.43
  91.0 1.0 reshape.311
  92.0 0.6 fusion.114
  93.5 1.2 fusion.45
  94.7 1.0 reshape.315
  95.7 1.5 fusion.115
  98.1 0.6 fusion.44
  99.0 6.0 %collective-permute-start = (bf16[64,3584]{1,0:T(8,128)(2,1)S(1)}, bf16[64,3584]{1,0:T(8,128)(2,1)S(1)}, u32[]{:S(2)}, u32[]{:S(2)}) collective-permute-start(bf16[64,3584]{1,0:T(8,128)(2,1)S(1)} %fusion.46), channel_id=1, source_target_pairs={{0,1},{1,2},{2,3},{4,5},{5,6},{6,7},{8,9},{9,10},{10,11},{12,13},{... | collective-permute-start | bytes 1376264 | tf_op jit(solution)/shard_map/ppermute | solution.py:14
  105.0 0.8 pad_maximum_fusion
  105.8 8.7 %collective-permute-done = bf16[64,3584]{1,0:T(8,128)(2,1)S(1)} collective-permute-done((bf16[64,3584]{1,0:T(8,128)(2,1)S(1)}, bf16[64,3584]{1,0:T(8,128)(2,1)S(1)}, u32[]{:S(2)}, u32[]{:S(2)}) %collective-permute-start) | collective-permute-done | bytes 458784 | tf_op jit(solution)/shard_map/ppermute | solution.py:14
  114.5 55.2 %reduce-scatter.4.cloned.1.call-done = f32[448,1024]{1,0:T(8,128)} async-done(((f32[3584,1024]{1,0:T(8,128)}), f32[448,1024]{1,0:T(8,128)}) %reduce-scatter.4.cloned.1.call-update) | async-done | bytes 1835024
  169.7 1.9 %copy.16 = f32[448,1024]{0,1:T(8,128)S(1)} copy(f32[448,1024]{1,0:T(8,128)} %reduce-scatter.4.cloned.1.call-done) | data formatting | bytes 3670016
  171.6 1.7 copy.14
  173.4 0.8 copy.34
  174.1 1.8 copy.35
  (85 shorter events, 10.6 us)
Async XLA Ops:
  7.2 26.8 %copy-start = (bf16[1,1,64,3584]{3,2,1,0:T(8,128)(2,1)S(1)}, bf16[1,1,64,3584]{3,2,1,0:T(8,128)(2,1)}, u32[]{:S(2)}) copy-start(bf16[1,1,64,3584]{3,2,1,0:T(8,128)(2,1)} %param.10) | copy-start | bytes 1376260
  7.2 4.8 %copy-start.6 = (bf16[1,1,64,3584]{3,2,1,0:T(8,128)(2,1)S(1)}, bf16[1,1,64,3584]{3,2,1,0:T(8,128)(2,1)}, u32[]{:S(2)}) copy-start(bf16[1,1,64,3584]{3,2,1,0:T(8,128)(2,1)} %param.12) | copy-start | bytes 1376260
  7.2 66.4 %all-gather.3.cloned.1.call-start = ((), (), s32[]{:S(2)}) async-start(), calls=%async_computation.1 | async-start | bytes 8257536 | tf_op jit(solution)/shard_map/all_gather | solution.py:109
  7.9 161.8 %reduce-scatter.4.cloned.1.call-start = ((), (), s32[]{:S(2)}) async-start(), calls=%async_computation.2 | async-start | bytes 16515072
  12.1 6.4 %copy-start.3 = (bf16[1,1,1024,1024]{3,2,1,0:T(8,128)(2,1)S(1)}, bf16[1,1,1024,1024]{3,2,1,0:T(8,128)(2,1)}, u32[]{:S(2)}) copy-start(bf16[1,1,1024,1024]{3,2,1,0:T(8,128)(2,1)} %param.13) | copy-start | bytes 6291460
  19.5 0.9 copy-start.11
  22.0 0.9 copy-start.9
  24.5 0.9 copy-start.8
  26.9 0.9 copy-start.10
  28.9 1.0 copy-start.19
  29.9 0.9 copy-start.20
  30.8 0.9 copy-start.21
  31.8 1.2 copy-start.22
  33.3 0.7 copy-start.4
  57.7 1.0 copy-start.7
  71.6 1.9 %copy-start.5 = (bf16[64,1024]{1,0:T(8,128)(2,1)S(1)}, bf16[64,1024]{1,0:T(8,128)(2,1)}, u32[]{:S(2)}) copy-start(bf16[64,1024]{1,0:T(8,128)(2,1)} %copy-done.4) | copy-start | bytes 393220
  73.6 9.9 %copy-start.2 = (bf16[1,3584,1024]{2,1,0:T(8,128)(2,1)S(1)}, bf16[1,3584,1024]{2,1,0:T(8,128)(2,1)}, u32[]{:S(2)}) copy-start(bf16[1,3584,1024]{2,1,0:T(8,128)(2,1)} %all-gather.3.cloned.1.call-done) | copy-start | bytes 22020100
  73.6 9.9 %copy-start.14 = (bf16[1,1,64,3584]{3,2,1,0:T(8,128)(2,1)S(1)}, bf16[1,1,64,3584]{3,2,1,0:T(8,128)(2,1)}, u32[]{:S(2)}) copy-start(bf16[1,1,64,3584]{3,2,1,0:T(8,128)(2,1)} %param.8) | copy-start | bytes 1376260
  81.8 3.1 %copy-start.13 = (bf16[448,128]{1,0:T(8,128)(2,1)S(1)}, bf16[448,128]{1,0:T(8,128)(2,1)}, u32[]{:S(2)}) copy-start(bf16[448,128]{1,0:T(8,128)(2,1)} %reshape.308) | copy-start | bytes 344068
  81.8 24.0 %collective-permute-start.1 = (bf16[64,3584]{1,0:T(8,128)(2,1)}, bf16[64,3584]{1,0:T(8,128)(2,1)}, u32[]{:S(2)}, u32[]{:S(2)}) collective-permute-start(bf16[64,3584]{1,0:T(8,128)(2,1)} %fusion.4), channel_id=1, source_target_pairs={{1,0},{2,1},{3,2},{5,4},{6,5},{7,6},{9,8},{10,9},{11,10},{13,12},{... | collective-permute-start | bytes 1376264 | tf_op jit(solution)/shard_map/ppermute | solution.py:14
  84.9 1.1 copy-start.15
  86.0 2.3 %copy-start.12 = (bf16[448,128]{1,0:T(8,128)(2,1)S(1)}, bf16[448,128]{1,0:T(8,128)(2,1)}, u32[]{:S(2)}) copy-start(bf16[448,128]{1,0:T(8,128)(2,1)} %reshape.310) | copy-start | bytes 344068
  88.9 0.9 copy-start.16
  92.6 0.8 copy-start.17
  97.3 0.9 copy-start.18
  99.0 15.5 %collective-permute-start = (bf16[64,3584]{1,0:T(8,128)(2,1)S(1)}, bf16[64,3584]{1,0:T(8,128)(2,1)S(1)}, u32[]{:S(2)}, u32[]{:S(2)}) collective-permute-start(bf16[64,3584]{1,0:T(8,128)(2,1)S(1)} %fusion.46), channel_id=1, source_target_pairs={{0,1},{1,2},{2,3},{4,5},{5,6},{6,7},{8,9},{9,10},{10,11},{12,13},{... | collective-permute-start | bytes 1376264 | tf_op jit(solution)/shard_map/ppermute | solution.py:14
  171.6 4.3 %copy-start.1 = (bf16[1,1,64,3584]{3,2,1,0:T(8,128)(2,1)S(1)}, bf16[1,1,64,3584]{3,2,1,0:T(8,128)(2,1)}, u32[]{:S(2)}) copy-start(bf16[1,1,64,3584]{3,2,1,0:T(8,128)(2,1)} %param.10) | copy-start | bytes 1376260
Sparse Core Ops, SparseCore 0:
  9.9 52.6 all-gather.2
  66.2 103.5 reduce-scatter.3
where the time goes:
time: 184 us; the launch traced here: 183 us
  waiting for transfers between devices  64.7 us (35%)
  local copies, waits for them, and re-layouts  45.9 us (25%)
  matrix products  41 us (22%)
  between operations  15.9 us (9%)
  starting transfers between devices  7.67 us (4%)
  other arithmetic  7.62 us (4%)
    unnamed x3, waiting for transfers between devices  55.9 us
    unnamed x51, local copies, waits for them, and re-layouts  26.8 us
    ppermute x2, waiting for transfers between devices, shifted(): lax.ppermute(value, axis, [(source, source + steps) for source in range(f...  8.73 us
    dot_general x1, matrix products, shards(): jnp.dot(columns.T, kv_grad, preferred_element_type=jnp.float32)  8.4 us
    dot_general x1, matrix products, shards(): jnp.dot(kv_grad, lax.all_gather(shard, 'dp', axis=0, tiled=True).T, prefe...  8.23 us
    ppermute x2, starting transfers between devices, shifted(): lax.ppermute(value, axis, [(source, source + steps) for source in range(f...  7.59 us
    dot_general x4, matrix products, backward_segment(): jnp.dot(dscore, key_head, preferred_element_type=jnp.float32) * scale  6.36 us
    dot_general x4, matrix products, forward_segment(): jnp.dot(probs, values[:, head * HD:(head + 1) * HD], preferred_element_ty...  4.14 us
  transfers between devices with their start and end apart: 4, of which 2 were waited for; matrix products, arithmetic and copies ran while one was open for 46% of the time, Pallas kernels for 0%

commit v1 on v0

--- a/solution.py
+++ b/solution.py
@@ -1,8 +1,11 @@
+import functools
 import math
 
 import jax
 import jax.numpy as jnp
 from jax import lax
+from jax.experimental import pallas as pl
+from jax.experimental.pallas import tpu as pltpu
 from jax.sharding import PartitionSpec as P
 
 HD = 128
@@ -126,10 +129,437 @@
     prev_grad = shifted(input_grad, "pipe", -1)
     return (next_act[None, None], grad_query[None, None], prev_grad[None, None], weight_grad[None])
 
+MESH = pl.DeviceIdType.MESH
+LANES = 128
+LOG2E = math.log2(math.e)
+
+
+def dot(a, b, dims):
+    return lax.dot_general(a, b, (dims, ((), ())), preferred_element_type=jnp.float32)
+
+
+def heads_of(ref, g, group):
+    width = group * HD
+    columns = ref[:, pl.ds(pl.multiple_of(g * width, LANES), width)]
+    return jnp.concatenate([columns[:, h * HD : (h + 1) * HD] for h in range(group)], axis=0)
+
+
+def heads_back(value, group):
+    seg = value.shape[0] // group
+    return jnp.concatenate([value[h * seg : (h + 1) * seg] for h in range(group)], axis=1)
+
+
+def fused(
+    chips,
+    stages,
+    len_ref,
+    fx_ref,
+    fq_ref,
+    bx_ref,
+    bq_ref,
+    bd_ref,
+    cache_ref,
+    w_ref,
+    next_ref,
+    gq_ref,
+    prev_ref,
+    wg_ref,
+    cache,
+    bq,
+    bd,
+    fq,
+    weight,
+    xf,
+    xb,
+    part,
+    own_in,
+    kvs,
+    kg,
+    high,
+    fout,
+    gq,
+    igrad,
+    terms,
+    other,
+    load_sem,
+    xf_s,
+    xf_r,
+    xb_s,
+    xb_r,
+    own_s,
+    own_r,
+    kg_s,
+    kg_r,
+    ig_s,
+    ig_r,
+    na_s,
+    na_r,
+    pair_s,
+    pair_r,
+    out_sem,
+):
+    seg, model = bq.shape
+    seq_len, both = cache.shape
+    half = both // 2
+    kv_heads = half // HD
+    group = model // half
+    window = model // chips
+    shard = w_ref.shape[0]
+    width = group * HD
+    low = seq_len - 2 * seg
+    scale = 1.0 / math.sqrt(HD)
+    me = lax.axis_index("dp")
+    stage = lax.axis_index("pipe")
+    chip, core = me // 2, me % 2
+    has_next, has_prev = stage < stages - 1, stage > 0
+
+    def at_chip(k):
+        return ((chip + k) % chips) * 2 + core
+
+    def columns_of(index):
+        return pl.ds(pl.multiple_of(index * window, LANES), window)
+
+    loads = [
+        pltpu.make_async_copy(source, target, load_sem.at[i])
+        for i, (source, target) in enumerate(
+            [
+                (bq_ref, bq),
+                (cache_ref, cache),
+                (bd_ref, bd),
+                (fx_ref.at[:, columns_of(chip)], xf.at[0]),
+                (w_ref, weight.at[pl.ds(pl.multiple_of(core * shard, 64), shard)]),
+                (fq_ref, fq),
+                (bx_ref.at[:, columns_of(chip)], xb.at[0]),
+            ]
+        )
+    ]
+    for load in loads:
+        load.start()
+
+    barrier = pltpu.get_barrier_semaphore()
+    sibling = chip * 2 + 1 - core
+    pl.semaphore_signal(barrier, inc=1, device_id={"dp": sibling}, device_id_type=MESH)
+    for k in range(1, chips):
+        pl.semaphore_signal(barrier, inc=1, device_id={"dp": at_chip(k)}, device_id_type=MESH)
+
+    @pl.when(has_next)
+    def _():
+        for k in range(chips):
+            pl.semaphore_signal(
+                barrier, inc=1, device_id={"dp": at_chip(k), "pipe": stage + 1}, device_id_type=MESH
+            )
+
+    @pl.when(has_prev)
+    def _():
+        for k in range(chips):
+            pl.semaphore_signal(
+                barrier, inc=1, device_id={"dp": at_chip(k), "pipe": stage - 1}, device_id_type=MESH
+            )
+
+    sides = (stage + stages - 1) // stages + (2 * stages - 2 - stage) // stages
+    pl.semaphore_wait(barrier, chips * (1 + sides))
+
+    def remote(source, target, send, recv, device):
+        return pltpu.make_async_remote_copy(
+            src_ref=source,
+            dst_ref=target,
+            send_sem=send,
+            recv_sem=recv,
+            device_id=device,
+            device_id_type=MESH,
+        )
+
+    def columns_copy(x_ref, slots, send, recv, k):
+        there = (chip + k) % chips
+        return remote(
+            x_ref.at[:, columns_of(there)], slots.at[k], send.at[k], recv.at[k], {"dp": at_chip(k)}
+        )
+
+    xf_copies = [columns_copy(fx_ref, xf, xf_s, xf_r, k) for k in range(1, chips)]
+    xb_copies = [columns_copy(bx_ref, xb, xb_s, xb_r, k) for k in range(1, chips)]
+    w_copy = remote(
+        w_ref,
+        weight.at[pl.ds(pl.multiple_of(core * shard, 64), shard)],
+        pair_s.at[0],
+        pair_r.at[0],
+        {"dp": sibling},
+    )
+    own_copies = [
+        remote(part.at[k], own_in.at[k], own_s.at[k], own_r.at[k], {"dp": at_chip(chips - k)})
+        for k in range(1, chips)
+    ]
+    kg_copies = [
+        remote(kg.at[0], kg.at[k], kg_s.at[k], kg_r.at[k], {"dp": at_chip(k)})
+        for k in range(1, chips)
+    ]
+    ig_copies = [
+        remote(
+            igrad.at[k],
+            prev_ref.at[:, columns_of(chip)],
+            ig_s.at[k],
+            ig_r.at[k],
+            {"dp": at_chip(chips - k), "pipe": stage - 1},
+        )
+        for k in range(chips)
+    ]
+
+    def next_copy(g):
+        piece = pl.ds(pl.multiple_of(g * width, LANES), width)
+        return remote(
+            fout.at[:, piece],
+            next_ref.at[:, piece],
+            na_s.at[g],
+            na_r.at[g],
+            {"dp": me, "pipe": stage + 1},
+        )
+
+    for copy in xf_copies:
+        copy.start()
+    w_copy.start()
+    for copy in xb_copies:
+        copy.start()
+
+    third, fourth = len_ref[0, 0, 2], len_ref[0, 0, 3]
+    start3 = seq_len - fourth
+    start2 = start3 - third
+    row = lax.broadcasted_iota(jnp.int32, (seg, 1), 0)
+    live2 = jnp.where(row < third, 1.0, 0.0)
+    live3 = jnp.where(row < fourth, 1.0, 0.0)
+    column = lax.broadcasted_iota(jnp.int32, (seg, seq_len - low), 1) + low
+    row_wide = lax.broadcasted_iota(jnp.int32, (seg, seq_len - low), 0)
+
+    def bias(start):
+        piece = jnp.where(column <= start + row_wide, 0.0, -1e30)
+        return jnp.concatenate([piece] * group, axis=0)
+
+    def softmax_parts(scores_low, scores_high, start):
+        scores_high = scores_high + bias(start)
+        top = jnp.maximum(
+            jnp.max(scores_low, axis=1, keepdims=True), jnp.max(scores_high, axis=1, keepdims=True)
+        )
+        raised_low = jnp.exp2((scores_low - top) * (scale * LOG2E))
+        raised_high = jnp.exp2((scores_high - top) * (scale * LOG2E))
+        total = jnp.sum(raised_low, axis=1, keepdims=True) + jnp.sum(
+            raised_high, axis=1, keepdims=True
+        )
+        return raised_low, raised_high, 1.0 / total
+
+    def lanes(start):
+        return pl.ds(pl.multiple_of(start, LANES), HD)
+
+    def project():
+        loads[3].wait()
+        loads[4].wait()
+        w_copy.wait()
+        for copy in xf_copies:
+            copy.wait()
+        product = dot(xf[...].reshape(chips * seg, window), weight[...], ((1,), (0,)))
+        part[...] = product.astype(jnp.bfloat16).reshape(part.shape)
+        for copy in own_copies:
+            copy.start()
+
+    loads[0].wait()
+    loads[1].wait()
+    loads[2].wait()
+
+    @pl.loop(0, kv_heads)
+    def _(g):
+        @pl.when(g == kv_heads // 2)
+        def _():
+            project()
+
+        query = heads_of(bq, g, group)
+        dout = heads_of(bd, g, group).astype(jnp.float32)
+        dout = (dout * jnp.concatenate([live2] * group, axis=0)).astype(jnp.bfloat16)
+        keys = cache[:, lanes(g * HD)]
+        values = cache[:, lanes(half + g * HD)]
+        scores = dot(query, keys, ((1,), (1,)))
+        e_low, e_high, inverse = softmax_parts(scores[:, :low], scores[:, low:], start2)
+        probs = jnp.concatenate([e_low, e_high], axis=1) * inverse
+        rounded = probs.astype(jnp.bfloat16)
+        mixed = dot(rounded, values, ((1,), (0,)))
+        delta = jnp.sum(dout.astype(jnp.float32) * mixed, axis=1, keepdims=True)
+        along = dot(dout, values, ((1,), (1,)))
+        dscore = (probs * (along - delta)).astype(jnp.bfloat16)
+        grad = dot(dscore, keys, ((1,), (0,))) * scale
+        gq[:, pl.ds(pl.multiple_of(g * width, LANES), width)] = heads_back(grad, group).astype(
+            jnp.bfloat16
+        )
+        key_grad = dot(dscore[:, low:], query, ((0,), (0,))) * scale
+        value_grad = dot(rounded[:, low:], dout, ((0,), (0,)))
+        kvs[:, lanes(g * HD)] = key_grad.astype(jnp.bfloat16)
+        kvs[:, lanes(half + g * HD)] = value_grad.astype(jnp.bfloat16)
+
+    pick = (column == start2 + row_wide) & (row_wide < third)
+    pick = jnp.where(pick, 1.0, 0.0).astype(jnp.bfloat16)
+    kg[0] = dot(pick, kvs[...], ((1,), (0,))).astype(jnp.bfloat16)
+    for copy in kg_copies:
+        copy.start()
+    gq_out = pltpu.make_async_copy(gq, gq_ref, out_sem.at[0])
+    gq_out.start()
+
+    for copy in own_copies:
+        copy.wait()
+    own = part[0].astype(jnp.float32)
+    for k in range(1, chips):
+        own = own + own_in[k].astype(jnp.float32)
+    own = own.astype(jnp.bfloat16)
+    spot = lax.broadcasted_iota(jnp.int32, (seq_len - low, seg), 0) + low
+    source = lax.broadcasted_iota(jnp.int32, (seq_len - low, seg), 1)
+    place = jnp.where(spot == start3 + source, 1.0, 0.0).astype(jnp.bfloat16)
+    moved = dot(place, own, ((1,), (0,)))
+    stored = lax.broadcasted_iota(jnp.int32, (seq_len - low, both), 0) + low < start3
+    high[...] = jnp.where(stored, cache[low:, :].astype(jnp.float32), moved).astype(jnp.bfloat16)
+    loads[5].wait()
+
+    @pl.loop(0, kv_heads)
+    def _(g):
+        query = heads_of(fq, g, group)
+        s_low = dot(query, cache[:low, lanes(g * HD)], ((1,), (1,)))
+        s_high = dot(query, high[:, lanes(g * HD)], ((1,), (1,)))
+        e_low, e_high, inverse = softmax_parts(s_low, s_high, start3)
+        mixed = dot(e_low.astype(jnp.bfloat16), cache[:low, lanes(half + g * HD)], ((1,), (0,)))
+        mixed = mixed + dot(
+            e_high.astype(jnp.bfloat16), high[:, lanes(half + g * HD)], ((1,), (0,))
+        )
+        mixed = mixed * (inverse * jnp.concatenate([live3] * group, axis=0))
+        fout[:, pl.ds(pl.multiple_of(g * width, LANES), width)] = heads_back(mixed, group).astype(
+            jnp.bfloat16
+        )
+
+        @pl.when(has_next)
+        def _():
+            next_copy(g).start()
+
+    for copy in kg_copies:
+        copy.wait()
+    gathered = kg[...].reshape(chips * seg, both)
+
+    @pl.when(has_prev)
+    def _():
+        grad = dot(gathered, weight[...], ((1,), (1,)))
+        igrad[...] = grad.astype(jnp.bfloat16).reshape(igrad.shape)
+        for copy in ig_copies:
+            copy.start()
+
+    loads[6].wait()
+    for copy in xb_copies:
+        copy.wait()
+    terms[...] = dot(xb[...].reshape(chips * seg, window), gathered, ((0,), (0,)))
+    t_copy = remote(
+        terms.at[pl.ds(pl.multiple_of((1 - core) * shard, 64), shard)],
+        other,
+        pair_s.at[1],
+        pair_r.at[1],
+        {"dp": sibling},
+    )
+    t_copy.start()
+
+    @pl.when(jnp.logical_not(has_prev))
+    def _():
+        igrad[...] = jnp.zeros_like(igrad)
+        fills = [
+            pltpu.make_async_copy(igrad.at[k], next_ref.at[:, columns_of(k)], ig_s.at[k])
+            for k in range(chips)
+        ]
+        for fill in fills:
+            fill.start()
+        for fill in fills:
+            fill.wait()
+
+    t_copy.wait()
+    other[...] = other[...] + terms[pl.ds(pl.multiple_of(core * shard, 64), shard), :]
+    wg_out = pltpu.make_async_copy(other, wg_ref, out_sem.at[1])
+    wg_out.start()
+
+    @pl.when(has_next)
+    def _():
+        for g in range(kv_heads):
+            next_copy(g).wait_send()
+        for k in range(chips):
+            ig_copies[k].wait_recv()
+
+    @pl.when(jnp.logical_not(has_next))
+    def _():
+        fout[...] = jnp.zeros_like(fout)
+        fill = pltpu.make_async_copy(fout, prev_ref, out_sem.at[2])
+        fill.start()
+        fill.wait()
+
+    @pl.when(has_prev)
+    def _():
+        for g in range(kv_heads):
+            next_copy(g).wait_recv()
+        for k in range(chips):
+            ig_copies[k].wait_send()
+
+    gq_out.wait()
+    wg_out.wait()
+
+
+def fused_shards(chips, stages, fwd_x, fwd_q, bwd_x, bwd_q, bwd_dout, cache_kv, kv_weight, lengths):
+    seg, model = fwd_x.shape[2:]
+    seq_len, both = cache_kv.shape[2:]
+    shard = kv_weight.shape[1]
+    window = model // chips
+    kv_heads = both // 2 // HD
+    wide = jax.ShapeDtypeStruct((seg, model), jnp.bfloat16)
+    vmem, dma = pltpu.VMEM, pltpu.SemaphoreType.DMA
+    bf16, f32 = jnp.bfloat16, jnp.float32
+    outs = pl.pallas_call(
+        functools.partial(fused, chips, stages),
+        out_shape=(wide, wide, wide, jax.ShapeDtypeStruct((shard, both), f32)),
+        in_specs=[pl.BlockSpec(memory_space=pltpu.SMEM)] + [pl.BlockSpec(memory_space=pl.ANY)] * 7,
+        out_specs=[pl.BlockSpec(memory_space=pl.ANY)] * 4,
+        scratch_shapes=[
+            vmem((seq_len, both), bf16),
+            vmem((seg, model), bf16),
+            vmem((seg, model), bf16),
+            vmem((seg, model), bf16),
+            vmem((2 * shard, both), bf16),
+            vmem((chips, seg, window), bf16),
+            vmem((chips, seg, window), bf16),
+            vmem((chips, seg, both), bf16),
+            vmem((chips, seg, both), bf16),
+            vmem((2 * seg, both), bf16),
+            vmem((chips, seg, both), bf16),
+            vmem((2 * seg, both), bf16),
+            vmem((seg, model), bf16),
+            vmem((seg, model), bf16),
+            vmem((chips, seg, window), bf16),
+            vmem((2 * shard, both), f32),
+            vmem((shard, both), f32),
+            dma((7,)),
+        ]
+        + [dma((chips,))] * 10
+        + [dma((kv_heads,)), dma((kv_heads,)), dma((2,)), dma((2,)), dma((3,))],
+        compiler_params=pltpu.CompilerParams(
+            collective_id=0, has_side_effects=True, vmem_limit_bytes=56 * 1024 * 1024
+        ),
+    )(
+        lengths,
+        fwd_x[0, 0],
+        fwd_q[0, 0],
+        bwd_x[0, 0],
+        bwd_q[0, 0],
+        bwd_dout[0, 0],
+        cache_kv[0, 0],
+        kv_weight[0],
+    )
+    next_act, grad_query, prev_grad, weight_grad = outs
+    return (next_act[None, None], grad_query[None, None], prev_grad[None, None], weight_grad[None])
+
 
 def solution(mesh):
+    ranks, stages = mesh.shape["dp"], mesh.shape["pipe"]
+
+    def body(fwd_x, *rest):
+        if ranks % 2 == 0 and fwd_x.shape[-1] % (ranks // 2 * LANES) == 0:
+            return fused_shards(ranks // 2, stages, fwd_x, *rest)
+        return shards(fwd_x, *rest)
+
     return jax.shard_map(
-        shards,
+        body,
         mesh=mesh,
         in_specs=(
             P("pipe", "dp", None, None),

time: 184 us -> 50.1 us (0.27)
  waiting for transfers between devices: 64.7 us -> 0 us
  Pallas kernels: 0 us -> 42.4 us
  matrix products: 41 us -> 0 us
  local copies, waits for them, and re-layouts: 45.9 us -> 6.81 us
  between operations: 15.9 us -> 0.65 us
  starting transfers between devices: 7.67 us -> 0 us
  other arithmetic: 7.62 us -> 0 us
    unnamed x3 -> x0, waiting for transfers between devices: 55.9 us -> none
    pallas_call x0 -> x1, Pallas kernels: none -> 42.4 us  [fused_shards(): pl.pallas_call(functools.partial(fused, chips, stages), out_shape=(wide,...]
    dot_general x35 -> x0, matrix products: 41 us -> none  [the longest x1 8.4 us: shards(): jnp.dot(columns.T, kv_grad, preferred_element_type=jnp.float32)]
    unnamed x51 -> x6, local copies, waits for them, and re-layouts: 26.8 us -> 6.81 us
    reshape x16 -> x0, local copies, waits for them, and re-layouts: 10.3 us -> none  [the longest x4 3.26 us: forward_segment(): pieces.append(mixed.reshape(seg, group * HD))]
    ppermute x2 -> x0, waiting for transfers between devices: 8.73 us -> none  [shifted(): lax.ppermute(value, axis, [(source, source + steps) for source in range(f...]
    ppermute x2 -> x0, starting transfers between devices: 7.59 us -> none  [shifted(): lax.ppermute(value, axis, [(source, source + steps) for source in range(f...]
    slice x6 -> x0, local copies, waits for them, and re-layouts: 5.07 us -> none  [the longest x2 1.89 us: forward_segment(): values = jnp.concatenate([cache[:, half:], own_kv[:, half:]], axis=0)]
  transfers between devices with their start and end apart: 4 -> 0, of which waited for: 2 -> 0; matrix products, arithmetic and copies ran while one was open for 46% -> 0% of each run, Pallas kernels for 0% -> 0%
where the time goes in v1:
time: 50.1 us; the launch traced here: 49.9 us
  Pallas kernels  42.4 us (85%)
  local copies, waits for them, and re-layouts  6.81 us (14%)
  between operations  0.65 us (1%)
    pallas_call x1, Pallas kernels, fused_shards(): pl.pallas_call(functools.partial(fused, chips, stages), out_shape=(wide,...  42.4 us
    unnamed x6, local copies, waits for them, and re-layouts  6.81 us

profile of v1, /device:TPU:0, one launch (start us, length us, event | category | flops | bytes accessed | tf_op | source)
XLA Modules:
  0.0 49.9 jit_solution(11862745313051963833)
XLA Ops:
  0.6 42.4 %shard_map.111 = (bf16[64,3584]{1,0:T(8,128)(2,1)}, bf16[64,3584]{1,0:T(8,128)(2,1)}, bf16[64,3584]{1,0:T(8,128)(2,1)}, f32[448,1024]{1,0:T(8,128)}) custom-call(s32[1,1,4]{2,1,0:T(1,128)} %len_ref.1, bf16[64,3584]{1,0:T(8,128)(2,1)} %bitcast.17, bf16[64,3584]{1,0:T(8,128)(2,1)} %bitcast.18, bf16[64,3584]{1,0:T(8,128)(2,1)} %bitcast.19, ...), custom_call_target="tpu_custom_call" | custom-call | tf_op jit(solution)/shard_map/pallas_call | solution.py:509
  43.1 0.0 copy-start
  43.1 1.9 %copy.16 = bf16[1,1,64,3584]{3,2,1,0:T(8,128)(2,1)} copy(bf16[1,1,64,3584]{3,2,1,0:T(8,128)(2,1)} %bitcast.16) | data formatting | bytes 917504
  45.0 1.8 %copy.17 = bf16[1,1,64,3584]{3,2,1,0:T(8,128)(2,1)} copy(bf16[1,1,64,3584]{3,2,1,0:T(8,128)(2,1)} %bitcast.15) | data formatting | bytes 917504
  46.8 1.8 %copy.18 = bf16[1,1,64,3584]{3,2,1,0:T(8,128)(2,1)} copy(bf16[1,1,64,3584]{3,2,1,0:T(8,128)(2,1)} %bitcast.14) | data formatting | bytes 917504
  48.6 0.0 copy-done
  48.6 1.2 %copy.19 = f32[1,448,1024]{2,1,0:T(8,128)} copy(f32[1,448,1024]{2,1,0:T(8,128)S(1)} %bitcast.12) | data formatting | bytes 3670016
Async XLA Ops:
  43.1 5.6 %copy-start = (f32[448,1024]{1,0:T(8,128)S(1)}, f32[448,1024]{1,0:T(8,128)}, u32[]{:S(2)}) copy-start(f32[448,1024]{1,0:T(8,128)} %get-tuple-element.11) | copy-start | bytes 5505028

commit v2 on v1

--- a/solution.py
+++ b/solution.py
@@ -173,7 +173,6 @@
     xb,
     part,
     own_in,
-    kvs,
     kg,
     high,
     fout,
@@ -292,6 +291,12 @@
         remote(kg.at[0], kg.at[k], kg_s.at[k], kg_r.at[k], {"dp": at_chip(k)})
         for k in range(1, chips)
     ]
+
+    def kg_piece(k, piece):
+        return remote(
+            kg.at[0, :, piece], kg.at[k, :, piece], kg_s.at[k], kg_r.at[k], {"dp": at_chip(k)}
+        )
+
     ig_copies = [
         remote(
             igrad.at[k],
@@ -316,8 +321,6 @@
     for copy in xf_copies:
         copy.start()
     w_copy.start()
-    for copy in xb_copies:
-        copy.start()
 
     third, fourth = len_ref[0, 0, 2], len_ref[0, 0, 3]
     start3 = seq_len - fourth
@@ -362,8 +365,16 @@
     loads[1].wait()
     loads[2].wait()
 
+    pick = (column == start2 + row_wide) & (row_wide < third)
+    pick = jnp.where(pick, 1.0, 0.0).astype(jnp.bfloat16)
+
     @pl.loop(0, kv_heads)
     def _(g):
+        @pl.when(g == 1)
+        def _():
+            for copy in xb_copies:
+                copy.start()
+
         @pl.when(g == kv_heads // 2)
         def _():
             project()
@@ -375,26 +386,28 @@
         values = cache[:, lanes(half + g * HD)]
         scores = dot(query, keys, ((1,), (1,)))
         e_low, e_high, inverse = softmax_parts(scores[:, :low], scores[:, low:], start2)
-        probs = jnp.concatenate([e_low, e_high], axis=1) * inverse
-        rounded = probs.astype(jnp.bfloat16)
-        mixed = dot(rounded, values, ((1,), (0,)))
-        delta = jnp.sum(dout.astype(jnp.float32) * mixed, axis=1, keepdims=True)
         along = dot(dout, values, ((1,), (1,)))
-        dscore = (probs * (along - delta)).astype(jnp.bfloat16)
-        grad = dot(dscore, keys, ((1,), (0,))) * scale
+        mixed = dot(e_low.astype(jnp.bfloat16), values[:low], ((1,), (0,)))
+        mixed = mixed + dot(e_high.astype(jnp.bfloat16), values[low:], ((1,), (0,)))
+        delta = jnp.sum(dout.astype(jnp.float32) * mixed, axis=1, keepdims=True) * inverse
+        d_low = e_low * (along[:, :low] - delta)
+        d_high = e_high * (along[:, low:] - delta)
+        grad = dot(d_low.astype(jnp.bfloat16), keys[:low], ((1,), (0,)))
+        grad = grad + dot(d_high.astype(jnp.bfloat16), keys[low:], ((1,), (0,)))
+        grad = grad * (inverse * scale)
+        key_grad = dot((d_high * inverse).astype(jnp.bfloat16), query, ((0,), (0,))) * scale
+        value_grad = dot((e_high * inverse).astype(jnp.bfloat16), dout, ((0,), (0,)))
+        for start, part_grad in ((g * HD, key_grad), (half + g * HD, value_grad)):
+            kg[0, :, lanes(start)] = dot(
+                pick, part_grad.astype(jnp.bfloat16), ((1,), (0,))
+            ).astype(jnp.bfloat16)
+        for k in range(1, chips):
+            kg_piece(k, lanes(g * HD)).start()
+            kg_piece(k, lanes(half + g * HD)).start()
         gq[:, pl.ds(pl.multiple_of(g * width, LANES), width)] = heads_back(grad, group).astype(
             jnp.bfloat16
         )
-        key_grad = dot(dscore[:, low:], query, ((0,), (0,))) * scale
-        value_grad = dot(rounded[:, low:], dout, ((0,), (0,)))
-        kvs[:, lanes(g * HD)] = key_grad.astype(jnp.bfloat16)
-        kvs[:, lanes(half + g * HD)] = value_grad.astype(jnp.bfloat16)
-
-    pick = (column == start2 + row_wide) & (row_wide < third)
-    pick = jnp.where(pick, 1.0, 0.0).astype(jnp.bfloat16)
-    kg[0] = dot(pick, kvs[...], ((1,), (0,))).astype(jnp.bfloat16)
-    for copy in kg_copies:
-        copy.start()
+
     gq_out = pltpu.make_async_copy(gq, gq_ref, out_sem.at[0])
     gq_out.start()
 
@@ -412,8 +425,38 @@
     high[...] = jnp.where(stored, cache[low:, :].astype(jnp.float32), moved).astype(jnp.bfloat16)
     loads[5].wait()
 
+    t_copy = remote(
+        terms.at[pl.ds(pl.multiple_of((1 - core) * shard, 64), shard)],
+        other,
+        pair_s.at[1],
+        pair_r.at[1],
+        {"dp": sibling},
+    )
+
+    def gradients():
+        for copy in kg_copies:
+            copy.wait()
+        gathered = kg[...].reshape(chips * seg, both)
+
+        @pl.when(has_prev)
+        def _():
+            grad = dot(gathered, weight[...], ((1,), (1,)))
+            igrad[...] = grad.astype(jnp.bfloat16).reshape(igrad.shape)
+            for copy in ig_copies:
+                copy.start()
+
+        loads[6].wait()
+        for copy in xb_copies:
+            copy.wait()
+        terms[...] = dot(xb[...].reshape(chips * seg, window), gathered, ((0,), (0,)))
+        t_copy.start()
+
     @pl.loop(0, kv_heads)
     def _(g):
+        @pl.when(g == 1)
+        def _():
+            gradients()
+
         query = heads_of(fq, g, group)
         s_low = dot(query, cache[:low, lanes(g * HD)], ((1,), (1,)))
         s_high = dot(query, high[:, lanes(g * HD)], ((1,), (1,)))
@@ -430,30 +473,6 @@
         @pl.when(has_next)
         def _():
             next_copy(g).start()
-
-    for copy in kg_copies:
-        copy.wait()
-    gathered = kg[...].reshape(chips * seg, both)
-
-    @pl.when(has_prev)
-    def _():
-        grad = dot(gathered, weight[...], ((1,), (1,)))
-        igrad[...] = grad.astype(jnp.bfloat16).reshape(igrad.shape)
-        for copy in ig_copies:
-            copy.start()
-
-    loads[6].wait()
-    for copy in xb_copies:
-        copy.wait()
-    terms[...] = dot(xb[...].reshape(chips * seg, window), gathered, ((0,), (0,)))
-    t_copy = remote(
-        terms.at[pl.ds(pl.multiple_of((1 - core) * shard, 64), shard)],
-        other,
-        pair_s.at[1],
-        pair_r.at[1],
-        {"dp": sibling},
-    )
-    t_copy.start()
 
     @pl.when(jnp.logical_not(has_prev))
     def _():
@@ -495,6 +514,22 @@
 
     gq_out.wait()
     wg_out.wait()
+
+
+def hand_over(*refs):
+    sources, targets, sem = refs[:4], refs[4:8], refs[8]
+    copies = []
+    for i in (3, 0, 1, 2):
+        rows = sources[i].shape[0] // 4
+        for j in range(4):
+            piece = pl.ds(j * rows, rows)
+            copies.append(
+                pltpu.make_async_copy(sources[i].at[piece], targets[i].at[piece], sem.at[i, j])
+            )
+    for copy in copies:
+        copy.start()
+    for copy in copies:
+        copy.wait()
 
 
 def fused_shards(chips, stages, fwd_x, fwd_q, bwd_x, bwd_q, bwd_dout, cache_kv, kv_weight, lengths):
@@ -521,7 +556,6 @@
             vmem((chips, seg, window), bf16),
             vmem((chips, seg, both), bf16),
             vmem((chips, seg, both), bf16),
-            vmem((2 * seg, both), bf16),
             vmem((chips, seg, both), bf16),
             vmem((2 * seg, both), bf16),
             vmem((seg, model), bf16),
@@ -546,7 +580,14 @@
         cache_kv[0, 0],
         kv_weight[0],
     )
-    next_act, grad_query, prev_grad, weight_grad = outs
+    next_act, grad_query, prev_grad, weight_grad = pl.pallas_call(
+        hand_over,
+        out_shape=tuple(jax.ShapeDtypeStruct(out.shape, out.dtype) for out in outs),
+        in_specs=[pl.BlockSpec(memory_space=pl.ANY)] * 4,
+        out_specs=[pl.BlockSpec(memory_space=pl.ANY)] * 4,
+        scratch_shapes=[dma((4, 4))],
+        compiler_params=pltpu.CompilerParams(vmem_limit_bytes=56 * 1024 * 1024),
+    )(*outs)
     return (next_act[None, None], grad_query[None, None], prev_grad[None, None], weight_grad[None])
 
 

time: 50.1 us -> 142 us (2.83)
  Pallas kernels: 42.4 us -> 141 us
  local copies, waits for them, and re-layouts: 6.81 us -> 0 us
    pallas_call x0 -> x1, Pallas kernels: none -> 98.5 us  [fused_shards(): pl.pallas_call(hand_over, out_shape=tuple((jax.ShapeDtypeStruct(out.shape...]
    unnamed x6 -> x0, local copies, waits for them, and re-layouts: 6.81 us -> none
where the time goes in v2:
time: 142 us; the launch traced here: 141 us
  Pallas kernels  141 us (99%)
    pallas_call x1, Pallas kernels, fused_shards(): pl.pallas_call(hand_over, out_shape=tuple((jax.ShapeDtypeStruct(out.shape...  98.5 us
    pallas_call x1, Pallas kernels, fused_shards(): pl.pallas_call(functools.partial(fused, chips, stages), out_shape=(wide,...  42.2 us

profile of v2, /device:TPU:0, one launch (start us, length us, event | category | flops | bytes accessed | tf_op | source)
XLA Modules:
  0.0 141.4 jit_solution(9033790434895732221)
XLA Ops:
  0.6 42.2 %shard_map.111 = (bf16[64,3584]{1,0:T(8,128)(2,1)}, bf16[64,3584]{1,0:T(8,128)(2,1)}, bf16[64,3584]{1,0:T(8,128)(2,1)}, f32[448,1024]{1,0:T(8,128)}) custom-call(s32[1,1,4]{2,1,0:T(1,128)} %len_ref.1, bf16[64,3584]{1,0:T(8,128)(2,1)} %bitcast.13, bf16[64,3584]{1,0:T(8,128)(2,1)} %bitcast.14, bf16[64,3584]{1,0:T(8,128)(2,1)} %bitcast.15, ...), custom_call_target="tpu_custom_call" | custom-call | tf_op jit(solution)/shard_map/pallas_call | solution.py:544
  42.8 98.5 %shard_map.112 = (bf16[64,3584]{1,0:T(8,128)(2,1)}, bf16[64,3584]{1,0:T(8,128)(2,1)}, bf16[64,3584]{1,0:T(8,128)(2,1)}, f32[448,1024]{1,0:T(8,128)}) custom-call(bf16[64,3584]{1,0:T(8,128)(2,1)} %get-tuple-element.12.refs_0_, bf16[64,3584]{1,0:T(8,128)(2,1)} %get-tuple-element.13.refs_1_, bf16[64,3584]{1,0:T(8,128)(2,1)} %get-tuple-element.14.refs_2_, ...), custom_call_target="tpu_custom_call" | custom-call | tf_op jit(solution)/shard_map/pallas_call | solution.py:583

commit v3 on v2

--- a/solution.py
+++ b/solution.py
@@ -176,10 +176,8 @@
     kg,
     high,
     fout,
-    gq,
     igrad,
     terms,
-    other,
     load_sem,
     xf_s,
     xf_r,
@@ -195,7 +193,6 @@
     na_r,
     pair_s,
     pair_r,
-    out_sem,
 ):
     seg, model = bq.shape
     seq_len, both = cache.shape
@@ -370,11 +367,6 @@
 
     @pl.loop(0, kv_heads)
     def _(g):
-        @pl.when(g == 1)
-        def _():
-            for copy in xb_copies:
-                copy.start()
-
         @pl.when(g == kv_heads // 2)
         def _():
             project()
@@ -387,9 +379,9 @@
         scores = dot(query, keys, ((1,), (1,)))
         e_low, e_high, inverse = softmax_parts(scores[:, :low], scores[:, low:], start2)
         along = dot(dout, values, ((1,), (1,)))
-        mixed = dot(e_low.astype(jnp.bfloat16), values[:low], ((1,), (0,)))
-        mixed = mixed + dot(e_high.astype(jnp.bfloat16), values[low:], ((1,), (0,)))
-        delta = jnp.sum(dout.astype(jnp.float32) * mixed, axis=1, keepdims=True) * inverse
+        delta = jnp.sum(e_low * along[:, :low], axis=1, keepdims=True)
+        delta = delta + jnp.sum(e_high * along[:, low:], axis=1, keepdims=True)
+        delta = delta * inverse
         d_low = e_low * (along[:, :low] - delta)
         d_high = e_high * (along[:, low:] - delta)
         grad = dot(d_low.astype(jnp.bfloat16), keys[:low], ((1,), (0,)))
@@ -404,12 +396,12 @@
         for k in range(1, chips):
             kg_piece(k, lanes(g * HD)).start()
             kg_piece(k, lanes(half + g * HD)).start()
-        gq[:, pl.ds(pl.multiple_of(g * width, LANES), width)] = heads_back(grad, group).astype(
+        gq_ref[:, pl.ds(pl.multiple_of(g * width, LANES), width)] = heads_back(grad, group).astype(
             jnp.bfloat16
         )
 
-    gq_out = pltpu.make_async_copy(gq, gq_ref, out_sem.at[0])
-    gq_out.start()
+    for copy in xb_copies:
+        copy.start()
 
     for copy in own_copies:
         copy.wait()
@@ -427,7 +419,7 @@
 
     t_copy = remote(
         terms.at[pl.ds(pl.multiple_of((1 - core) * shard, 64), shard)],
-        other,
+        wg_ref,
         pair_s.at[1],
         pair_r.at[1],
         {"dp": sibling},
@@ -445,9 +437,11 @@
             for copy in ig_copies:
                 copy.start()
 
+    def weight_terms():
         loads[6].wait()
         for copy in xb_copies:
             copy.wait()
+        gathered = kg[...].reshape(chips * seg, both)
         terms[...] = dot(xb[...].reshape(chips * seg, window), gathered, ((0,), (0,)))
         t_copy.start()
 
@@ -456,6 +450,10 @@
         @pl.when(g == 1)
         def _():
             gradients()
+
+        @pl.when(g == 2)
+        def _():
+            weight_terms()
 
         query = heads_of(fq, g, group)
         s_low = dot(query, cache[:low, lanes(g * HD)], ((1,), (1,)))
@@ -476,20 +474,14 @@
 
     @pl.when(jnp.logical_not(has_prev))
     def _():
-        igrad[...] = jnp.zeros_like(igrad)
-        fills = [
-            pltpu.make_async_copy(igrad.at[k], next_ref.at[:, columns_of(k)], ig_s.at[k])
-            for k in range(chips)
-        ]
-        for fill in fills:
-            fill.start()
-        for fill in fills:
-            fill.wait()
+        next_ref[...] = jnp.zeros_like(next_ref)
+
+    @pl.when(jnp.logical_not(has_next))
+    def _():
+        prev_ref[...] = jnp.zeros_like(prev_ref)
 
     t_copy.wait()
-    other[...] = other[...] + terms[pl.ds(pl.multiple_of(core * shard, 64), shard), :]
-    wg_out = pltpu.make_async_copy(other, wg_ref, out_sem.at[1])
-    wg_out.start()
+    wg_ref[...] = wg_ref[...] + terms[pl.ds(pl.multiple_of(core * shard, 64), shard), :]
 
     @pl.when(has_next)
     def _():
@@ -498,13 +490,6 @@
         for k in range(chips):
             ig_copies[k].wait_recv()
 
-    @pl.when(jnp.logical_not(has_next))
-    def _():
-        fout[...] = jnp.zeros_like(fout)
-        fill = pltpu.make_async_copy(fout, prev_ref, out_sem.at[2])
-        fill.start()
-        fill.wait()
-
     @pl.when(has_prev)
     def _():
         for g in range(kv_heads):
@@ -512,20 +497,13 @@
         for k in range(chips):
             ig_copies[k].wait_send()
 
-    gq_out.wait()
-    wg_out.wait()
-
 
 def hand_over(*refs):
     sources, targets, sem = refs[:4], refs[4:8], refs[8]
-    copies = []
-    for i in (3, 0, 1, 2):
-        rows = sources[i].shape[0] // 4
-        for j in range(4):
-            piece = pl.ds(j * rows, rows)
-            copies.append(
-                pltpu.make_async_copy(sources[i].at[piece], targets[i].at[piece], sem.at[i, j])
-            )
+    copies = [
+        pltpu.make_async_copy(source, target, sem.at[i])
+        for i, (source, target) in enumerate(zip(sources, targets))
+    ]
     for copy in copies:
         copy.start()
     for copy in copies:
@@ -538,14 +516,14 @@
     shard = kv_weight.shape[1]
     window = model // chips
     kv_heads = both // 2 // HD
-    wide = jax.ShapeDtypeStruct((seg, model), jnp.bfloat16)
+    wide = pltpu.VMEM((seg, model), jnp.bfloat16)
     vmem, dma = pltpu.VMEM, pltpu.SemaphoreType.DMA
     bf16, f32 = jnp.bfloat16, jnp.float32
     outs = pl.pallas_call(
         functools.partial(fused, chips, stages),
-        out_shape=(wide, wide, wide, jax.ShapeDtypeStruct((shard, both), f32)),
+        out_shape=(wide, wide, wide, pltpu.VMEM((shard, both), f32)),
         in_specs=[pl.BlockSpec(memory_space=pltpu.SMEM)] + [pl.BlockSpec(memory_space=pl.ANY)] * 7,
-        out_specs=[pl.BlockSpec(memory_space=pl.ANY)] * 4,
+        out_specs=[pl.BlockSpec(memory_space=pltpu.VMEM)] * 4,
         scratch_shapes=[
             vmem((seq_len, both), bf16),
             vmem((seg, model), bf16),
@@ -559,16 +537,14 @@
             vmem((chips, seg, both), bf16),
             vmem((2 * seg, both), bf16),
             vmem((seg, model), bf16),
-            vmem((seg, model), bf16),
             vmem((chips, seg, window), bf16),
             vmem((2 * shard, both), f32),
-            vmem((shard, both), f32),
             dma((7,)),
         ]
         + [dma((chips,))] * 10
-        + [dma((kv_heads,)), dma((kv_heads,)), dma((2,)), dma((2,)), dma((3,))],
+        + [dma((kv_heads,)), dma((kv_heads,)), dma((2,)), dma((2,))],
         compiler_params=pltpu.CompilerParams(
-            collective_id=0, has_side_effects=True, vmem_limit_bytes=56 * 1024 * 1024
+            collective_id=0, has_side_effects=True, vmem_limit_bytes=59 * 1024 * 1024
         ),
     )(
         lengths,
@@ -583,10 +559,10 @@
     next_act, grad_query, prev_grad, weight_grad = pl.pallas_call(
         hand_over,
         out_shape=tuple(jax.ShapeDtypeStruct(out.shape, out.dtype) for out in outs),
-        in_specs=[pl.BlockSpec(memory_space=pl.ANY)] * 4,
+        in_specs=[pl.BlockSpec(memory_space=pltpu.VMEM)] * 4,
         out_specs=[pl.BlockSpec(memory_space=pl.ANY)] * 4,
-        scratch_shapes=[dma((4, 4))],
-        compiler_params=pltpu.CompilerParams(vmem_limit_bytes=56 * 1024 * 1024),
+        scratch_shapes=[dma((4,))],
+        compiler_params=pltpu.CompilerParams(vmem_limit_bytes=16 * 1024 * 1024),
     )(*outs)
     return (next_act[None, None], grad_query[None, None], prev_grad[None, None], weight_grad[None])
 

time: 142 us -> 40.2 us (0.28)
  the two profiles are of different devices: /device:TPU:0 before, /device:TPU:26 now
where the time goes in v3:
time: 40.2 us; the launch traced here: 40.1 us
  Pallas kernels  39.4 us (98%)
  between operations  0.64 us (2%)
    pallas_call x1, Pallas kernels, fused_shards(): pl.pallas_call(functools.partial(fused, chips, stages), out_shape=(wide,...  37.7 us
    pallas_call x1, Pallas kernels, fused_shards(): pl.pallas_call(hand_over, out_shape=tuple((jax.ShapeDtypeStruct(out.shape...  1.72 us

profile of v3, /device:TPU:26, one launch (start us, length us, event | category | flops | bytes accessed | tf_op | source)
XLA Modules:
  0.0 40.1 jit_solution(4496270671104707872)
XLA Ops:
  0.6 37.7 %shard_map.111 = (bf16[64,3584]{1,0:T(8,128)(2,1)S(1)}, bf16[64,3584]{1,0:T(8,128)(2,1)S(1)}, bf16[64,3584]{1,0:T(8,128)(2,1)S(1)}, f32[448,1024]{1,0:T(8,128)S(1)}) custom-call(s32[1,1,4]{2,1,0:T(1,128)} %len_ref.1, bf16[64,3584]{1,0:T(8,128)(2,1)} %bitcast.13, bf16[64,3584]{1,0:T(8,128)(2,1)} %bitcast.14, bf16[64,3584]{1,0:T(8,128)(2,1)} %bitcast.15, ...), custom_call_target="tpu_custom_call" | custom-call | tf_op jit(solution)/shard_map/pallas_call | solution.py:522
  38.4 1.7 %shard_map.112 = (bf16[64,3584]{1,0:T(8,128)(2,1)}, bf16[64,3584]{1,0:T(8,128)(2,1)}, bf16[64,3584]{1,0:T(8,128)(2,1)}, f32[448,1024]{1,0:T(8,128)}) custom-call(bf16[64,3584]{1,0:T(8,128)(2,1)S(1)} %get-tuple-element.12.refs_0_, bf16[64,3584]{1,0:T(8,128)(2,1)S(1)} %get-tuple-element.13.refs_1_, bf16[64,3584]{1,0:T(8,128)(2,1)S(1)} %get-tuple-element.14.refs_2_, ...), custom_call_target="tpu_custom_call" | custom-call | tf_op jit(solution)/shard_map/pallas_call | solution.py:559

commit v4 on v3

--- a/solution.py
+++ b/solution.py
@@ -140,7 +140,7 @@
 
 def heads_of(ref, g, group):
     width = group * HD
-    columns = ref[:, pl.ds(pl.multiple_of(g * width, LANES), width)]
+    columns = ref[:, pl.ds(g * width, width)]
     return jnp.concatenate([columns[:, h * HD : (h + 1) * HD] for h in range(group)], axis=0)
 
 
@@ -306,7 +306,7 @@
     ]
 
     def next_copy(g):
-        piece = pl.ds(pl.multiple_of(g * width, LANES), width)
+        piece = pl.ds(g * width, width)
         return remote(
             fout.at[:, piece],
             next_ref.at[:, piece],
@@ -345,7 +345,7 @@
         return raised_low, raised_high, 1.0 / total
 
     def lanes(start):
-        return pl.ds(pl.multiple_of(start, LANES), HD)
+        return pl.ds(start, HD)
 
     def project():
         loads[3].wait()
@@ -365,28 +365,39 @@
     pick = (column == start2 + row_wide) & (row_wide < third)
     pick = jnp.where(pick, 1.0, 0.0).astype(jnp.bfloat16)
 
-    @pl.loop(0, kv_heads)
-    def _(g):
-        @pl.when(g == kv_heads // 2)
+    def forward_begin(g):
+        query = heads_of(fq, g, group)
+        return query, dot(query, cache[:low, lanes(g * HD)], ((1,), (1,)))
+
+    def forward_end(g, query, s_low):
+        s_high = dot(query, high[:, lanes(g * HD)], ((1,), (1,)))
+        e_low, e_high, inverse = softmax_parts(s_low, s_high, start3)
+        mixed = dot(e_low.astype(jnp.bfloat16), cache[:low, lanes(half + g * HD)], ((1,), (0,)))
+        mixed = mixed + dot(
+            e_high.astype(jnp.bfloat16), high[:, lanes(half + g * HD)], ((1,), (0,))
+        )
+        mixed = mixed * (inverse * jnp.concatenate([live3] * group, axis=0))
+        fout[:, pl.ds(g * width, width)] = heads_back(mixed, group).astype(jnp.bfloat16)
+
+        @pl.when(has_next)
         def _():
-            project()
-
+            next_copy(g).start()
+
+    def backward_begin(g):
         query = heads_of(bq, g, group)
         dout = heads_of(bd, g, group).astype(jnp.float32)
         dout = (dout * jnp.concatenate([live2] * group, axis=0)).astype(jnp.bfloat16)
-        keys = cache[:, lanes(g * HD)]
-        values = cache[:, lanes(half + g * HD)]
-        scores = dot(query, keys, ((1,), (1,)))
+        scores = dot(query, cache[:, lanes(g * HD)], ((1,), (1,)))
+        along = dot(dout, cache[:, lanes(half + g * HD)], ((1,), (1,)))
+        return query, dout, scores, along
+
+    def backward_end(g, query, dout, scores, along):
         e_low, e_high, inverse = softmax_parts(scores[:, :low], scores[:, low:], start2)
-        along = dot(dout, values, ((1,), (1,)))
         delta = jnp.sum(e_low * along[:, :low], axis=1, keepdims=True)
         delta = delta + jnp.sum(e_high * along[:, low:], axis=1, keepdims=True)
         delta = delta * inverse
         d_low = e_low * (along[:, :low] - delta)
         d_high = e_high * (along[:, low:] - delta)
-        grad = dot(d_low.astype(jnp.bfloat16), keys[:low], ((1,), (0,)))
-        grad = grad + dot(d_high.astype(jnp.bfloat16), keys[low:], ((1,), (0,)))
-        grad = grad * (inverse * scale)
         key_grad = dot((d_high * inverse).astype(jnp.bfloat16), query, ((0,), (0,))) * scale
         value_grad = dot((e_high * inverse).astype(jnp.bfloat16), dout, ((0,), (0,)))
         for start, part_grad in ((g * HD, key_grad), (half + g * HD, value_grad)):
@@ -396,9 +407,20 @@
         for k in range(1, chips):
             kg_piece(k, lanes(g * HD)).start()
             kg_piece(k, lanes(half + g * HD)).start()
-        gq_ref[:, pl.ds(pl.multiple_of(g * width, LANES), width)] = heads_back(grad, group).astype(
-            jnp.bfloat16
-        )
+        keys = cache[:, lanes(g * HD)]
+        grad = dot(d_low.astype(jnp.bfloat16), keys[:low], ((1,), (0,)))
+        grad = grad + dot(d_high.astype(jnp.bfloat16), keys[low:], ((1,), (0,)))
+        grad = grad * (inverse * scale)
+        gq_ref[:, pl.ds(g * width, width)] = heads_back(grad, group).astype(jnp.bfloat16)
+
+    loads[5].wait()
+    state = backward_begin(0)
+    for g in range(kv_heads):
+        later = backward_begin(g + 1) if g + 1 < kv_heads else forward_begin(0)
+        backward_end(g, *state)
+        state = later
+        if g == kv_heads // 2 - 1:
+            project()
 
     for copy in xb_copies:
         copy.start()
@@ -415,7 +437,6 @@
     moved = dot(place, own, ((1,), (0,)))
     stored = lax.broadcasted_iota(jnp.int32, (seq_len - low, both), 0) + low < start3
     high[...] = jnp.where(stored, cache[low:, :].astype(jnp.float32), moved).astype(jnp.bfloat16)
-    loads[5].wait()
 
     t_copy = remote(
         terms.at[pl.ds(pl.multiple_of((1 - core) * shard, 64), shard)],
@@ -445,32 +466,14 @@
         terms[...] = dot(xb[...].reshape(chips * seg, window), gathered, ((0,), (0,)))
         t_copy.start()
 
-    @pl.loop(0, kv_heads)
-    def _(g):
-        @pl.when(g == 1)
-        def _():
+    for g in range(kv_heads):
+        later = forward_begin(g + 1) if g + 1 < kv_heads else None
+        forward_end(g, *state)
+        state = later
+        if g == 0:
             gradients()
-
-        @pl.when(g == 2)
-        def _():
+        if g == 1:
             weight_terms()
-
-        query = heads_of(fq, g, group)
-        s_low = dot(query, cache[:low, lanes(g * HD)], ((1,), (1,)))
-        s_high = dot(query, high[:, lanes(g * HD)], ((1,), (1,)))
-        e_low, e_high, inverse = softmax_parts(s_low, s_high, start3)
-        mixed = dot(e_low.astype(jnp.bfloat16), cache[:low, lanes(half + g * HD)], ((1,), (0,)))
-        mixed = mixed + dot(
-            e_high.astype(jnp.bfloat16), high[:, lanes(half + g * HD)], ((1,), (0,))
-        )
-        mixed = mixed * (inverse * jnp.concatenate([live3] * group, axis=0))
-        fout[:, pl.ds(pl.multiple_of(g * width, LANES), width)] = heads_back(mixed, group).astype(
-            jnp.bfloat16
-        )
-
-        @pl.when(has_next)
-        def _():
-            next_copy(g).start()
 
     @pl.when(jnp.logical_not(has_prev))
     def _():

time: 40.2 us -> 40.3 us (level)
  no operation moved by 1% of the time
where the time goes in v4:
time: 40.3 us; the launch traced here: 40.1 us
  Pallas kernels  39.5 us (98%)
  between operations  0.64 us (2%)
    pallas_call x1, Pallas kernels, fused_shards(): pl.pallas_call(functools.partial(fused, chips, stages), out_shape=(wide,...  37.8 us
    pallas_call x1, Pallas kernels, fused_shards(): pl.pallas_call(hand_over, out_shape=tuple((jax.ShapeDtypeStruct(out.shape...  1.72 us

profile of v4, /device:TPU:26, one launch (start us, length us, event | category | flops | bytes accessed | tf_op | source)
XLA Modules:
  0.0 40.1 jit_solution(4965740334813245775)
XLA Ops:
  0.6 37.8 %shard_map.111 = (bf16[64,3584]{1,0:T(8,128)(2,1)S(1)}, bf16[64,3584]{1,0:T(8,128)(2,1)S(1)}, bf16[64,3584]{1,0:T(8,128)(2,1)S(1)}, f32[448,1024]{1,0:T(8,128)S(1)}) custom-call(s32[1,1,4]{2,1,0:T(1,128)} %len_ref.1, bf16[64,3584]{1,0:T(8,128)(2,1)} %bitcast.13, bf16[64,3584]{1,0:T(8,128)(2,1)} %bitcast.14, bf16[64,3584]{1,0:T(8,128)(2,1)} %bitcast.15, ...), custom_call_target="tpu_custom_call" | custom-call | tf_op jit(solution)/shard_map/pallas_call | solution.py:525
  38.4 1.7 %shard_map.112 = (bf16[64,3584]{1,0:T(8,128)(2,1)}, bf16[64,3584]{1,0:T(8,128)(2,1)}, bf16[64,3584]{1,0:T(8,128)(2,1)}, f32[448,1024]{1,0:T(8,128)}) custom-call(bf16[64,3584]{1,0:T(8,128)(2,1)S(1)} %get-tuple-element.12.refs_0_, bf16[64,3584]{1,0:T(8,128)(2,1)S(1)} %get-tuple-element.13.refs_1_, bf16[64,3584]{1,0:T(8,128)(2,1)S(1)} %get-tuple-element.14.refs_2_, ...), custom_call_target="tpu_custom_call" | custom-call | tf_op jit(solution)/shard_map/pallas_call | solution.py:562

commit v5 on v4

--- a/solution.py
+++ b/solution.py
@@ -422,6 +422,35 @@
         if g == kv_heads // 2 - 1:
             project()
 
+    t_copy = remote(
+        terms.at[pl.ds(pl.multiple_of((1 - core) * shard, 64), shard)],
+        wg_ref,
+        pair_s.at[1],
+        pair_r.at[1],
+        {"dp": sibling},
+    )
+
+    def input_gradient(first, count):
+        @pl.when(has_prev)
+        def _():
+            held = kg[first : first + count].reshape(count * seg, both)
+            grad = dot(held, weight[...], ((1,), (1,))).astype(jnp.bfloat16)
+            igrad[first : first + count] = grad.reshape(count, seg, window)
+            for copy in ig_copies[first : first + count]:
+                copy.start()
+
+    def weight_terms():
+        loads[6].wait()
+        for copy in xb_copies:
+            copy.wait()
+        gathered = kg[...].reshape(chips * seg, both)
+        terms[...] = dot(xb[...].reshape(chips * seg, window), gathered, ((0,), (0,)))
+        t_copy.start()
+
+    input_gradient(0, 1)
+    for copy in kg_copies:
+        copy.wait()
+    input_gradient(1, chips - 1)
     for copy in xb_copies:
         copy.start()
 
@@ -438,41 +467,11 @@
     stored = lax.broadcasted_iota(jnp.int32, (seq_len - low, both), 0) + low < start3
     high[...] = jnp.where(stored, cache[low:, :].astype(jnp.float32), moved).astype(jnp.bfloat16)
 
-    t_copy = remote(
-        terms.at[pl.ds(pl.multiple_of((1 - core) * shard, 64), shard)],
-        wg_ref,
-        pair_s.at[1],
-        pair_r.at[1],
-        {"dp": sibling},
-    )
-
-    def gradients():
-        for copy in kg_copies:
-            copy.wait()
-        gathered = kg[...].reshape(chips * seg, both)
-
-        @pl.when(has_prev)
-        def _():
-            grad = dot(gathered, weight[...], ((1,), (1,)))
-            igrad[...] = grad.astype(jnp.bfloat16).reshape(igrad.shape)
-            for copy in ig_copies:
-                copy.start()
-
-    def weight_terms():
-        loads[6].wait()
-        for copy in xb_copies:
-            copy.wait()
-        gathered = kg[...].reshape(chips * seg, both)
-        terms[...] = dot(xb[...].reshape(chips * seg, window), gathered, ((0,), (0,)))
-        t_copy.start()
-
     for g in range(kv_heads):
         later = forward_begin(g + 1) if g + 1 < kv_heads else None
         forward_end(g, *state)
         state = later
-        if g == 0:
-            gradients()
-        if g == 1:
+        if g == kv_heads - 2:
             weight_terms()
 
     @pl.when(jnp.logical_not(has_prev))

time: 40.3 us -> 43 us (1.067)
  the two profiles are of different devices: /device:TPU:26 before, /device:TPU:0 now
where the time goes in v5:
time: 43 us; the launch traced here: 42.8 us
  Pallas kernels  42.2 us (98%)
  between operations  0.64 us (1%)
    pallas_call x1, Pallas kernels, fused_shards(): pl.pallas_call(functools.partial(fused, chips, stages), out_shape=(wide,...  40.5 us
    pallas_call x1, Pallas kernels, fused_shards(): pl.pallas_call(hand_over, out_shape=tuple((jax.ShapeDtypeStruct(out.shape...  1.72 us

profile of v5, /device:TPU:0, one launch (start us, length us, event | category | flops | bytes accessed | tf_op | source)
XLA Modules:
  0.0 42.8 jit_solution(18304060604842120567)
XLA Ops:
  0.6 40.5 %shard_map.111 = (bf16[64,3584]{1,0:T(8,128)(2,1)S(1)}, bf16[64,3584]{1,0:T(8,128)(2,1)S(1)}, bf16[64,3584]{1,0:T(8,128)(2,1)S(1)}, f32[448,1024]{1,0:T(8,128)S(1)}) custom-call(s32[1,1,4]{2,1,0:T(1,128)} %len_ref.1, bf16[64,3584]{1,0:T(8,128)(2,1)} %bitcast.13, bf16[64,3584]{1,0:T(8,128)(2,1)} %bitcast.14, bf16[64,3584]{1,0:T(8,128)(2,1)} %bitcast.15, ...), custom_call_target="tpu_custom_call" | custom-call | tf_op jit(solution)/shard_map/pallas_call | solution.py:524
  41.1 1.7 %shard_map.112 = (bf16[64,3584]{1,0:T(8,128)(2,1)}, bf16[64,3584]{1,0:T(8,128)(2,1)}, bf16[64,3584]{1,0:T(8,128)(2,1)}, f32[448,1024]{1,0:T(8,128)}) custom-call(bf16[64,3584]{1,0:T(8,128)(2,1)S(1)} %get-tuple-element.12.refs_0_, bf16[64,3584]{1,0:T(8,128)(2,1)S(1)} %get-tuple-element.13.refs_1_, bf16[64,3584]{1,0:T(8,128)(2,1)S(1)} %get-tuple-element.14.refs_2_, ...), custom_call_target="tpu_custom_call" | custom-call | tf_op jit(solution)/shard_map/pallas_call | solution.py:561

commit v6 on v5

--- a/solution.py
+++ b/solution.py
@@ -178,6 +178,8 @@
     fout,
     igrad,
     terms,
+    term_out,
+    term_in,
     load_sem,
     xf_s,
     xf_r,
@@ -421,10 +423,12 @@
         state = later
         if g == kv_heads // 2 - 1:
             project()
+            for copy in xb_copies:
+                copy.start()
 
     t_copy = remote(
-        terms.at[pl.ds(pl.multiple_of((1 - core) * shard, 64), shard)],
-        wg_ref,
+        term_out,
+        term_in,
         pair_s.at[1],
         pair_r.at[1],
         {"dp": sibling},
@@ -445,14 +449,14 @@
             copy.wait()
         gathered = kg[...].reshape(chips * seg, both)
         terms[...] = dot(xb[...].reshape(chips * seg, window), gathered, ((0,), (0,)))
+        theirs = terms[pl.ds(pl.multiple_of((1 - core) * shard, 64), shard), :]
+        term_out[...] = theirs.astype(jnp.bfloat16)
         t_copy.start()
 
     input_gradient(0, 1)
     for copy in kg_copies:
         copy.wait()
     input_gradient(1, chips - 1)
-    for copy in xb_copies:
-        copy.start()
 
     for copy in own_copies:
         copy.wait()
@@ -471,7 +475,7 @@
         later = forward_begin(g + 1) if g + 1 < kv_heads else None
         forward_end(g, *state)
         state = later
-        if g == kv_heads - 2:
+        if g == 0:
             weight_terms()
 
     @pl.when(jnp.logical_not(has_prev))
@@ -483,7 +487,8 @@
         prev_ref[...] = jnp.zeros_like(prev_ref)
 
     t_copy.wait()
-    wg_ref[...] = wg_ref[...] + terms[pl.ds(pl.multiple_of(core * shard, 64), shard), :]
+    mine = terms[pl.ds(pl.multiple_of(core * shard, 64), shard), :]
+    wg_ref[...] = mine + term_in[...].astype(jnp.float32)
 
     @pl.when(has_next)
     def _():
@@ -541,6 +546,8 @@
             vmem((seg, model), bf16),
             vmem((chips, seg, window), bf16),
             vmem((2 * shard, both), f32),
+            vmem((shard, both), bf16),
+            vmem((shard, both), bf16),
             dma((7,)),
         ]
         + [dma((chips,))] * 10

time: 43 us -> 42.6 us (level)
  Pallas kernels: 42.2 us -> 41.6 us
    pallas_call x1, Pallas kernels: 40.5 us -> 39.9 us  [fused_shards(): pl.pallas_call(functools.partial(fused, chips, stages), out_shape=(wide,...]
where the time goes in v6:
time: 42.6 us; the launch traced here: 42.2 us
  Pallas kernels  41.6 us (98%)
  between operations  0.64 us (2%)
    pallas_call x1, Pallas kernels, fused_shards(): pl.pallas_call(functools.partial(fused, chips, stages), out_shape=(wide,...  39.9 us
    pallas_call x1, Pallas kernels, fused_shards(): pl.pallas_call(hand_over, out_shape=tuple((jax.ShapeDtypeStruct(out.shape...  1.72 us

profile of v6, /device:TPU:0, one launch (start us, length us, event | category | flops | bytes accessed | tf_op | source)
XLA Modules:
  0.0 42.2 jit_solution(6301021447695245841)
XLA Ops:
  0.6 39.9 %shard_map.111 = (bf16[64,3584]{1,0:T(8,128)(2,1)S(1)}, bf16[64,3584]{1,0:T(8,128)(2,1)S(1)}, bf16[64,3584]{1,0:T(8,128)(2,1)S(1)}, f32[448,1024]{1,0:T(8,128)S(1)}) custom-call(s32[1,1,4]{2,1,0:T(1,128)} %len_ref.1, bf16[64,3584]{1,0:T(8,128)(2,1)} %bitcast.13, bf16[64,3584]{1,0:T(8,128)(2,1)} %bitcast.14, bf16[64,3584]{1,0:T(8,128)(2,1)} %bitcast.15, ...), custom_call_target="tpu_custom_call" | custom-call | tf_op jit(solution)/shard_map/pallas_call | solution.py:529
  40.5 1.7 %shard_map.112 = (bf16[64,3584]{1,0:T(8,128)(2,1)}, bf16[64,3584]{1,0:T(8,128)(2,1)}, bf16[64,3584]{1,0:T(8,128)(2,1)}, f32[448,1024]{1,0:T(8,128)}) custom-call(bf16[64,3584]{1,0:T(8,128)(2,1)S(1)} %get-tuple-element.12.refs_0_, bf16[64,3584]{1,0:T(8,128)(2,1)S(1)} %get-tuple-element.13.refs_1_, bf16[64,3584]{1,0:T(8,128)(2,1)S(1)} %get-tuple-element.14.refs_2_, ...), custom_call_target="tpu_custom_call" | custom-call | tf_op jit(solution)/shard_map/pallas_call | solution.py:568
